TPU v7x, 512 devices: a whole 4x4x16 slice. The times are simulated.
512 devices in a mesh: wide: 64 (over z, y), narrow: 8 (over x, core).
Axes of the slice: x: 4, y: 4, z: 16, core: 2. Of those that a mesh axis runs over, the one named last changes fastest.
Arguments:
- coeffs: bfloat16 [65536, 9216], P('wide', 'narrow'), may hold values from -6 to 6
- earlier: bfloat16 [65536, 2048], P('wide', 'narrow'), may hold values from -6 to 6
- inv_tiles: float32 [4, 128, 128], replicated, may hold values from -0.041666667 to 0.041666667
- piv_local: int32 [512], replicated, may hold values from 0 to 1023
- piv_owner: int32 [512, 1], replicated, may hold values from 0 to 63; in each aligned block of 512 rows (0 to 511, 512 to 1023, ...) at most 24 rows name the same one
Outputs:
- new_columns: float32 [65536, 512], P('wide', 'narrow')
Inputs may be any that keep to these rules, and one draw needn't show every extreme that they name: `piv_owner`: each index of wide owns at most 24 of the 512 pivots, and some index owns exactly 24.
All inputs are finite; a program needn't handle non-finite values.
Results may differ from a plain program's by a relative error of at most 0.0003.
Values may be sent and summed in bfloat16 or wider, within the bound.
A program may use at most 64 MiB of HBM per device.

v0:
```python
import jax
import jax.numpy as jnp
from jax import lax
from jax.sharding import PartitionSpec as P


def panel_factor(density, diag_block, inv_tiles):
    block_size = inv_tiles.shape[1]
    piv_parts = []
    new_parts = []
    for block_index in range(inv_tiles.shape[0]):
        low_edge = block_index * block_size
        high_edge = low_edge + block_size
        piv_rest = diag_block[:, low_edge:high_edge]
        new_rest = density[:, low_edge:high_edge]
        if block_index > 0:
            piv_left = jnp.concatenate(piv_parts, axis=1)
            new_left = jnp.concatenate(new_parts, axis=1)
            coupling = piv_left[low_edge:high_edge]
            piv_rest = piv_rest - jnp.dot(piv_left, coupling.T, precision=lax.Precision.HIGHEST)
            new_rest = new_rest - jnp.dot(new_left, coupling.T, precision=lax.Precision.HIGHEST)
        piv_parts.append(jnp.dot(piv_rest, inv_tiles[block_index], precision=lax.Precision.HIGHEST))
        new_parts.append(jnp.dot(new_rest, inv_tiles[block_index], precision=lax.Precision.HIGHEST))
    return jnp.concatenate(new_parts, axis=1)


def on_device(coeffs, earlier, inv_tiles, piv_local, piv_owner):
    owners = piv_owner[:, 0]
    mine = owners == lax.axis_index("wide")
    pick_coeffs = jnp.where(mine[:, None], coeffs[piv_local].astype(jnp.float32), 0.0)
    pick_earlier = jnp.where(mine[:, None], earlier[piv_local].astype(jnp.float32), 0.0)
    summed_coeffs, summed_earlier = lax.psum((pick_coeffs, pick_earlier), "wide")
    pivot_coeffs = summed_coeffs.astype(jnp.bfloat16)
    pivot_earlier = summed_earlier.astype(jnp.bfloat16)
    partial_value = jnp.einsum(
        "ro,po->rp", coeffs, pivot_coeffs, preferred_element_type=jnp.float32
    )
    partial_value = partial_value - jnp.einsum(
        "ro,po->rp", earlier, pivot_earlier, preferred_element_type=jnp.float32
    )
    density = lax.psum_scatter(partial_value, "narrow", scatter_dimension=0, tiled=True)
    diag_part = jnp.einsum(
        "qo,po->qp", pivot_coeffs, pivot_coeffs, preferred_element_type=jnp.float32
    )
    diag_part = diag_part - jnp.einsum(
        "qo,po->qp", pivot_earlier, pivot_earlier, preferred_element_type=jnp.float32
    )
    diag_block = lax.psum(diag_part, "narrow")
    factor = panel_factor(density, diag_block, inv_tiles)
    return lax.all_to_all(factor, "narrow", split_axis=1, concat_axis=0, tiled=True)


def solution(mesh):
    return jax.shard_map(
        on_device,
        mesh=mesh,
        in_specs=(P("wide", "narrow"), P("wide", "narrow"), P(), P(), P()),
        out_specs=P("wide", "narrow"),
        check_vma=False,
    )
```

profile of v0, /device:TPU:1, one launch (start us, length us, event | category | flops | bytes accessed | tf_op | source)
XLA Modules:
  0.0 476.3 jit_solution(7588075105497317978)
XLA Ops:
  6.5 0.0 copy-start
  6.5 0.0 all-reduce.4.cloned.1.call-start
  6.5 0.8 compare_select_fusion
  7.4 0.7 compare_reduce_fusion
  8.1 2.7 gather_fusion.1
  10.8 0.9 convert_select_fusion.1
  11.7 0.0 copy-done
  11.7 2.1 gather_fusion
  13.8 1.6 convert_select_fusion
  15.4 265.6 %all-reduce.5 = (bf16[512,1152]{1,0:T(8,128)(2,1)}, bf16[512,256]{1,0:T(8,128)(2,1)S(1)}) all-reduce(f32[512,1152]{1,0:T(8,128)} %convert_select_fusion, f32[512,256]{1,0:T(8,128)} %convert_select_fusion.1), channel_id=1, replica_groups=mesh['wide'=64,'narrow'=8] {'wide'}, use_global_device_ids=true, to_apply=%region_0.1 | all-reduce | flops 720896 | bytes 4325376 | tf_op jit(solution)/shard_map/psum | solution.py:32
  281.0 2.5 fusion.46
  283.5 1.3 convolution_subtract_fusion
  284.8 0.0 all-reduce.4.cloned.1.call-update
  284.9 0.0 copy-start.1
  284.9 0.0 reduce-scatter.2.cloned.1.call-start
  284.9 2.9 fusion.47
  287.8 0.0 copy-done.1
  287.8 1.9 subtract_bitcast_fusion
  289.7 0.0 copy-start.2
  289.7 0.0 reduce-scatter.2.cloned.1.call-update
  289.7 118.5 %all-reduce.4.cloned.1.call-done = f32[512,512]{1,0:T(8,128)} async-done(((f32[512,512]{1,0:T(8,128)}), f32[512,512]{1,0:T(8,128)}) %all-reduce.4.cloned.1.call-update) | async-done | bytes 1048592 | tf_op jit(solution)/shard_map/psum | solution.py:48
  408.1 0.0 copy-done.2
  408.2 1.4 fusion.7
  409.5 1.5 convolution_subtract_fusion.2
  411.1 0.4 fusion.28
  411.5 1.9 convolution_subtract_fusion.1
  413.4 0.4 fusion.24
  413.9 37.6 %reduce-scatter.2.cloned.1.call-done = f32[128,512]{0,1:T(8,128)} async-done(((f32[1024,512]{0,1:T(8,128)}), f32[128,512]{0,1:T(8,128)}) %reduce-scatter.2.cloned.1.call-update) | async-done | bytes 262160 | tf_op jit(solution)/shard_map/reduce_scatter | solution.py:41
  451.5 1.1 fusion.20
  452.6 1.1 convolution_subtract_fusion.4
  453.8 0.3 fusion.30
  454.1 1.2 convolution_subtract_fusion.3
  455.3 0.3 fusion.26
  455.6 1.3 convolution_subtract_fusion.5
  456.9 0.3 fusion.22
  457.3 11.5 %all_to_all.19 = f32[128,8,64]{0,2,1:T(8,128)S(1)} all-to-all(f32[128,8,64]{0,2,1:T(8,128)S(1)} %bitcast.42), channel_id=1, replica_groups=mesh['wide'=64,'narrow'=8] {'narrow'}, dimensions={1} | all-to-all | bytes 524288 | tf_op jit(solution)/shard_map/all_to_all | solution.py:50
  468.7 0.7 copy_bitcast_fusion
  (2 shorter events, 0.0 us)
Async XLA Ops:
  6.5 5.1 %copy-start = (bf16[1024,1152]{1,0:T(8,128)(2,1)S(1)}, bf16[1024,1152]{1,0:T(8,128)(2,1)}, u32[]{:S(2)}) copy-start(bf16[1024,1152]{1,0:T(8,128)(2,1)} %param.5) | copy-start | bytes 7077892
  6.5 401.6 %all-reduce.4.cloned.1.call-start = ((), (), s32[]{:S(2)}) async-start(), calls=%async_computation.3 | async-start | bytes 2097152 | tf_op jit(solution)/shard_map/psum | solution.py:48
  284.9 2.9 copy-start.1
  284.9 166.6 %reduce-scatter.2.cloned.1.call-start = ((), (), s32[]{:S(2)}) async-start(), calls=%async_computation.2 | async-start | bytes 2359296 | tf_op jit(solution)/shard_map/reduce_scatter | solution.py:41
  289.7 118.5 %copy-start.2 = (f32[4,128,128]{2,1,0:T(8,128)S(1)}, f32[4,128,128]{2,1,0:T(8,128)}, u32[]{:S(2)}) copy-start(f32[4,128,128]{2,1,0:T(8,128)} %param.7) | copy-start | bytes 786436
Sparse Core Ops, SparseCore 0:
  285.0 123.1 all-reduce.3
  411.0 40.4 reduce-scatter.1
where the time goes:
time: 477 us; the launch traced here: 476 us
  blocking collectives  277 us (58%)
  waiting for transfers between devices  156 us (33%)
  matrix products  19.9 us (4%)
  between operations  13.5 us (3%)
  local copies, waits for them, and re-layouts  5.51 us (1%)
    psum x1, blocking collectives, on_device(): lax.psum((pick_coeffs, pick_earlier), 'wide')  266 us
    psum x1, waiting for transfers between devices, on_device(): diag_block = lax.psum(diag_part, 'narrow')  118 us
    reduce_scatter x1, waiting for transfers between devices, on_device(): lax.psum_scatter(partial_value, 'narrow', scatter_dimension=0, tiled=True)  37.6 us
    all_to_all x1, blocking collectives, on_device(): lax.all_to_all(factor, 'narrow', split_axis=1, concat_axis=0, tiled=True)  11.5 us
  transfers between devices with their start and end apart: 2, of which 2 were waited for; matrix products, arithmetic and copies ran while one was open for 2% of the time, Pallas kernels for 0%

commit v1 on v0

v1 whole, which is shorter than its diff:
```python
import jax
import jax.numpy as jnp
from jax import lax
from jax.experimental import pallas as pl
from jax.experimental.pallas import tpu as pltpu
from jax.sharding import PartitionSpec as P

MESH = pl.DeviceIdType.MESH
F32 = jnp.float32
BF16 = jnp.bfloat16
HIGH = lax.Precision.HIGHEST

NPIV = 512
BLK = 128
NY = 4
NZ = 16
NX = 4
CAP = 24
SLOT = 32
GROUP = CAP * NY
PIECES = 3
QCOL = PIECES * 128
LOW = ((1, 0), (2, 0), (2, 1), (3, 0), (3, 1), (3, 2))
SKEW = 2


def dot(a, b, precision=None):
    return lax.dot_general(a, b, (((1,), (0,)), ((), ())), precision=precision, preferred_element_type=F32)


def dot_nt(a, b, precision=None):
    return lax.dot_general(a, b, (((1,), (1,)), ((), ())), precision=precision, preferred_element_type=F32)


def ones_where(cond):
    return jnp.where(cond, 1.0, 0.0).astype(F32)


def kernel(coeffs, earlier, inv, own_col, own_row, loc_row, out,
           sel, ygot, ring, rows, hot,
           diag, diag_core, diag_x, diag_all,
           part_send, part_mine, part_got, half_a, half_b, from_left, from_right,
           pack, got,
           y1s, y1r, zs, zr, y2s, y2r, dcs, dcr, dxs, dxr, dys, dyr, pcs, pcr, xas, xar, xbs, xbr, os_, or_):
    wide = lax.axis_index("wide")
    narrow = lax.axis_index("narrow")
    z, y = wide // NY, wide % NY
    x, core = narrow // 2, narrow % 2
    z_next, z_prev = (z + 1) % NZ, (z + NZ - 1) % NZ
    y_next, y_prev = (y + 1) % NY, (y + NY - 1) % NY
    x_next, x_prev, x_far = (x + 1) % NX, (x + 3) % NX, (x + 2) % NX

    def at(zz=z, yy=y, xx=x, cc=core):
        return {"wide": zz * NY + yy, "narrow": xx * 2 + cc}

    def remote(src, dst, send_sem, recv_sem, device):
        return pltpu.make_async_remote_copy(
            src_ref=src, dst_ref=dst, send_sem=send_sem, recv_sem=recv_sem,
            device_id=device, device_id_type=MESH)

    other = 1 - core
    ys = [(y + d) % NY for d in (1, 3, 2)]
    xs = [x_next, x_prev, x_far]

    barrier = pltpu.get_barrier_semaphore()
    peers = [at(zz=z_next), at(zz=z_prev), at(cc=other)]
    peers += [at(yy=v, cc=c) for v in ys for c in (core, other)]
    peers += [at(xx=v, cc=c) for v in xs for c in (core, other)]
    for peer in peers:
        pl.semaphore_signal(barrier, inc=1, device_id=peer, device_id_type=MESH)

    owners = own_row[...]
    owner_col = own_col[...]
    before = lax.broadcasted_iota(jnp.int32, (NPIV, NPIV), 0) < lax.broadcasted_iota(jnp.int32, (NPIV, NPIV), 1)
    same_owner = owner_col == owners
    slot_row = jnp.sum(ones_where(before & same_owner), axis=0, keepdims=True)
    slots = lax.broadcasted_iota(jnp.int32, (SLOT, NPIV), 0).astype(F32)
    held = (slots == slot_row) & (owners == wide)
    place = jnp.sum(jnp.where(held, loc_row[...].astype(F32) + 1.0, 0.0), axis=1, keepdims=True) - 1.0
    pick = ones_where(lax.broadcasted_iota(jnp.int32, (SLOT, 1024), 1).astype(F32) == place).astype(BF16)
    n_coeff, n_early = coeffs.shape[-1], earlier.shape[-1]
    sel[:, :n_coeff] = dot(pick, coeffs[...].reshape(1024, n_coeff)).astype(BF16)
    sel[:, n_coeff:n_coeff + n_early] = dot(pick, earlier[...].reshape(1024, n_early)).astype(BF16)
    rest = NY * QCOL - n_coeff - n_early
    sel[:, n_coeff + n_early:] = jnp.zeros((SLOT, rest), BF16)

    pl.semaphore_wait(barrier, len(peers))

    def quarter(v):
        return pl.ds(pl.multiple_of(v * QCOL, 128), QCOL)

    spread = [remote(sel.at[:, quarter(v)], ygot.at[y], y1s.at[i], y1r.at[i], at(yy=v)) for i, v in enumerate(ys)]
    for copy in spread:
        copy.start()
    ygot[y] = sel[:, quarter(y)]

    z_row, z_col = owners // NY, owner_col // NY
    same_z = z_col == z_row
    rank_row = jnp.sum(ones_where(before & same_z), axis=0, keepdims=True)
    after = lax.broadcasted_iota(jnp.int32, (NPIV, NPIV), 1) < lax.broadcasted_iota(jnp.int32, (NPIV, NPIV), 0)
    rank_col = jnp.sum(ones_where(after & same_z), axis=1, keepdims=True)
    slot_col = jnp.sum(ones_where(after & same_owner), axis=1, keepdims=True)
    ranks = lax.broadcasted_iota(jnp.int32, (GROUP, NPIV), 0).astype(F32)
    to_rank = ones_where((ranks == rank_row) & (z_row == z)).astype(BF16)
    source = (owner_col % NY * SLOT).astype(F32) + slot_col
    from_slot = ones_where((lax.broadcasted_iota(jnp.int32, (NPIV, NY * SLOT), 1).astype(F32) == source) & (z_col == z)).astype(BF16)
    compact = dot(to_rank, from_slot).astype(BF16)
    target = (z_col * GROUP).astype(F32) + rank_col
    hot[...] = ones_where(lax.broadcasted_iota(jnp.int32, (NPIV, NZ * GROUP), 1).astype(F32) == target).astype(BF16)

    for copy in spread:
        copy.wait_recv()
    chunk = dot(compact, ygot[...].reshape(NY * SLOT, QCOL)).astype(BF16)

    def chunk_rows(v):
        return pl.ds(pl.multiple_of(v * GROUP, 16), GROUP)

    for g in range(PIECES):
        ring[g, chunk_rows(z), :] = chunk[:, g * 128:(g + 1) * 128]

    def ring_copy(way, step, g):
        origin = (z - (step - 1) + NZ) % NZ if way == 0 else (z + (step - 1)) % NZ
        ref = ring.at[g, chunk_rows(origin), :]
        return remote(ref, ref, zs.at[way, step - 1, g], zr.at[way, step - 1, g], at(zz=z_next if way == 0 else z_prev))

    def steps_of(way, g):
        longer = 0 if g % 2 == 0 else 1
        return NZ // 2 if way == longer else NZ // 2 - 1

    copies = {(way, s, g): ring_copy(way, s, g) for g in range(PIECES) for way in (0, 1) for s in range(1, steps_of(way, g) + 1)}

    def column(v, g):
        return pl.ds(pl.multiple_of(v * QCOL + g * 128, 128), 128)

    def whole_copy(way, g):
        ref = rows.at[:, column(y, g)]
        return remote(ref, ref, y2s.at[way, g], y2r.at[way, g], at(yy=y_next if way == 0 else y_prev))

    def pass_on(way, g):
        ref = rows.at[pl.ds(way * 256, 256), column(y_prev if way == 0 else y_next, g)]
        return remote(ref, ref, y2s.at[2 + way, g], y2r.at[2 + way, g], at(yy=y_next if way == 0 else y_prev))

    whole = {(way, g): whole_copy(way, g) for way in (0, 1) for g in range(PIECES)}
    passed = {(way, g): pass_on(way, g) for way in (0, 1) for g in range(PIECES)}

    def finish_piece(g):
        for way in (0, 1):
            copies[way, steps_of(way, g), g].wait_recv()
        rows[:, column(y, g)] = dot(hot[...], ring[g]).astype(BF16)
        for way in (0, 1):
            whole[way, g].start()

    for tick in range(1, NZ // 2 + 1 + SKEW * (PIECES - 1) + 1):
        for g in range(PIECES):
            step = tick - SKEW * g
            for way in (0, 1):
                if 1 <= step <= steps_of(way, g):
                    if step > 1:
                        copies[way, step - 1, g].wait_recv()
                    copies[way, step, g].start()
            if step == NZ // 2 + 1:
                finish_piece(g)
    for g in range(PIECES):
        for way in (0, 1):
            whole[way, g].wait_recv()
            passed[way, g].start()
    for g in range(PIECES):
        for way in (0, 1):
            passed[way, g].wait_recv()

    def pivots(low, high):
        return rows[low:high, :n_coeff], rows[low:high, n_coeff:n_coeff + n_early]

    for b in (1, 2, 3):
        left_c, left_e = pivots(b * BLK, (b + 1) * BLK)
        right_c, right_e = pivots(0, b * BLK)
        value = dot_nt(left_c, right_c) - dot_nt(left_e, right_e)
        for c in range(b):
            diag[LOW.index((b, c))] = value[:, c * BLK:(c + 1) * BLK]

    to_core = remote(diag.at[pl.ds(other * 3, 3)], diag_core, dcs, dcr, at(cc=other))
    to_core.start()

    piv_c, piv_e = pivots(0, NPIV)

    def partial(c):
        left_c = coeffs[:, c].reshape(NX * BLK, n_coeff)
        left_e = earlier[:, c].reshape(NX * BLK, n_early)
        return (dot_nt(left_c, piv_c) - dot_nt(left_e, piv_e)).reshape(NX, BLK, NPIV)

    part_send[...] = partial(other)
    order = [x_far, x_next, x_prev, x]
    part_copies = [remote(part_send.at[v], part_got.at[v], pcs.at[i], pcr.at[i], at(cc=other)) for i, v in enumerate(order)]
    for copy in part_copies:
        copy.start()

    def quarter_rows(v):
        return pl.ds(pl.multiple_of(v * 32, 32), 32)

    to_core.wait_recv()
    diag_x[x] = diag[pl.ds(core * 3, 3), quarter_rows(y)] + diag_core[:, quarter_rows(y)]
    diag_xs = [remote(diag_x.at[x], diag_x.at[x], dxs.at[i], dxr.at[i], at(xx=v)) for i, v in enumerate(xs)]
    for copy in diag_xs:
        copy.start()

    part_mine[...] = partial(core)

    for copy in diag_xs:
        copy.wait()
    diag_all[pl.ds(core * 3, 3), quarter_rows(y)] = diag_x[0] + diag_x[1] + diag_x[2] + diag_x[3]
    spot = diag_all.at[pl.ds(core * 3, 3), quarter_rows(y)]
    kin = [at(yy=v, cc=c) for v in ys for c in (core, other)] + [at(cc=other)]
    diag_ys = [remote(spot, spot, dys.at[i], dyr.at[i], who) for i, who in enumerate(kin)]
    for copy in diag_ys:
        copy.start()

    for v, copy in zip(order, part_copies):
        copy.wait_recv()
        part_mine[v] = part_mine[v] + part_got[v]
        if v is x_far:
            first_a = remote(part_mine.at[x_far, pl.ds(0, 64)], half_a, xas.at[0], xar.at[0], at(xx=x_next))
            first_b = remote(part_mine.at[x_far, pl.ds(64, 64)], half_b, xas.at[1], xar.at[1], at(xx=x_prev))
            first_a.start()
            first_b.start()
    next_now = remote(part_mine.at[x_next, pl.ds(64, 64)], from_left.at[pl.ds(64, 64)], xbs.at[0], xbr.at[0], at(xx=x_next))
    prev_now = remote(part_mine.at[x_prev, pl.ds(0, 64)], from_right.at[pl.ds(0, 64)], xbs.at[1], xbr.at[1], at(xx=x_prev))
    next_now.start()
    prev_now.start()
    first_a.wait_recv()
    part_mine[x_next, 0:64, :] = part_mine[x_next, 0:64, :] + half_a[...]
    next_then = remote(part_mine.at[x_next, pl.ds(0, 64)], from_left.at[pl.ds(0, 64)], xbs.at[2], xbr.at[2], at(xx=x_next))
    next_then.start()
    first_b.wait_recv()
    part_mine[x_prev, 64:128, :] = part_mine[x_prev, 64:128, :] + half_b[...]
    prev_then = remote(part_mine.at[x_prev, pl.ds(64, 64)], from_right.at[pl.ds(64, 64)], xbs.at[3], xbr.at[3], at(xx=x_prev))
    prev_then.start()

    for copy in diag_ys:
        copy.wait()
    low = {}
    for c in range(3):
        below = list(range(c + 1, 4))
        rest_rows = jnp.concatenate([diag_all[LOW.index((b, c))] for b in below], axis=0)
        for d in range(c):
            rest_rows = rest_rows - dot_nt(jnp.concatenate([low[b, d] for b in below], axis=0), low[c, d], HIGH)
        solved = dot(rest_rows, inv[c], HIGH)
        for i, b in enumerate(below):
            low[b, c] = solved[i * BLK:(i + 1) * BLK]

    for copy in (next_now, prev_now, next_then, prev_then):
        copy.wait_recv()
    density = part_mine[x] + from_left[...] + from_right[...]
    new = []
    outs = []
    for b in range(4):
        rest_cols = density[:, b * BLK:(b + 1) * BLK]
        for d in range(b):
            rest_cols = rest_cols - dot_nt(new[d], low[b, d], HIGH)
        value = dot(rest_cols, inv[b], HIGH)
        new.append(value)
        pack[2 * b] = jnp.concatenate([value[0:64, 0:64], value[64:128, 0:64]], axis=1)
        pack[2 * b + 1] = jnp.concatenate([value[0:64, 64:128], value[64:128, 64:128]], axis=1)
    home = [(x, other)] + [(v, c) for v in xs for c in (core, other)]
    for i, (xx, cc) in enumerate(home):
        copy = remote(pack.at[xx * 2 + cc], got.at[narrow], os_.at[i], or_.at[i], at(xx=xx, cc=cc))
        copy.start()
        outs.append(copy)
    got[narrow] = pack[narrow]
    for copy in outs:
        copy.wait_recv()
    for n in range(2 * NX):
        value = got[n]
        out[n * BLK:n * BLK + 64, :] = value[:, 0:64]
        out[n * BLK + 64:(n + 1) * BLK, :] = value[:, 64:128]

    for copy in spread + list(copies.values()) + list(whole.values()) + list(passed.values()):
        copy.wait_send()
    for copy in [to_core, first_a, first_b, next_now, prev_now, next_then, prev_then] + part_copies + outs:
        copy.wait_send()


def on_device(coeffs, earlier, inv_tiles, piv_local, piv_owner):
    n_coeff, n_early = coeffs.shape[1], earlier.shape[1]
    dma = pltpu.SemaphoreType.DMA
    vmem = pltpu.VMEM
    return pl.pallas_call(
        kernel,
        out_shape=jax.ShapeDtypeStruct((1024, NPIV // (2 * NX)), F32),
        in_specs=[pl.BlockSpec(memory_space=pltpu.VMEM)] * 6,
        out_specs=pl.BlockSpec(memory_space=pltpu.VMEM),
        scratch_shapes=[
            vmem((SLOT, NY * QCOL), BF16),
            vmem((NY, SLOT, QCOL), BF16),
            vmem((PIECES, NZ * GROUP, 128), BF16),
            vmem((NPIV, NY * QCOL), BF16),
            vmem((NPIV, NZ * GROUP), BF16),
            vmem((6, BLK, BLK), F32),
            vmem((3, BLK, BLK), F32),
            vmem((NX, 3, 32, BLK), F32),
            vmem((6, BLK, BLK), F32),
            vmem((NX, BLK, NPIV), F32),
            vmem((NX, BLK, NPIV), F32),
            vmem((NX, BLK, NPIV), F32),
            vmem((64, NPIV), F32),
            vmem((64, NPIV), F32),
            vmem((BLK, NPIV), F32),
            vmem((BLK, NPIV), F32),
            vmem((2 * NX, 64, BLK), F32),
            vmem((2 * NX, 64, BLK), F32),
            dma((3,)), dma((3,)),
            dma((2, NZ // 2, PIECES)), dma((2, NZ // 2, PIECES)),
            dma((4, PIECES)), dma((4, PIECES)),
            dma, dma,
            dma((3,)), dma((3,)),
            dma((7,)), dma((7,)),
            dma((4,)), dma((4,)),
            dma((2,)), dma((2,)),
            dma((4,)), dma((4,)),
            dma((7,)), dma((7,)),
        ],
        compiler_params=pltpu.CompilerParams(
            collective_id=0, has_side_effects=True, vmem_limit_bytes=56 * 1024 * 1024),
        cost_estimate=pl.CostEstimate(flops=4_000_000_000, bytes_accessed=4_000_000, transcendentals=0),
    )(coeffs.reshape(NX, 2, BLK, n_coeff), earlier.reshape(NX, 2, BLK, n_early), inv_tiles,
      piv_owner, piv_owner.reshape(1, NPIV), piv_local.reshape(1, NPIV))


def solution(mesh):
    return jax.shard_map(
        on_device,
        mesh=mesh,
        in_specs=(P("wide", "narrow"), P("wide", "narrow"), P(), P(), P()),
        out_specs=P("wide", "narrow"),
        check_vma=False,
    )
```

time: 477 us -> 99.3 us (0.21)
  blocking collectives: 277 us -> 0 us
  waiting for transfers between devices: 156 us -> 0 us
  Pallas kernels: 0 us -> 95.7 us
  matrix products: 19.9 us -> 0 us
  between operations: 13.5 us -> 0.01 us
    psum x1 -> x0, blocking collectives: 266 us -> none  [on_device(): lax.psum((pick_coeffs, pick_earlier), 'wide')]
    psum x1 -> x0, waiting for transfers between devices: 118 us -> none  [on_device(): diag_block = lax.psum(diag_part, 'narrow')]
    pallas_call x0 -> x1, Pallas kernels: none -> 95.7 us  [on_device(): pl.pallas_call(kernel, out_shape=jax.ShapeDtypeStruct((1024, NPIV // (2 *...]
    reduce_scatter x1 -> x0, waiting for transfers between devices: 37.6 us -> none  [on_device(): lax.psum_scatter(partial_value, 'narrow', scatter_dimension=0, tiled=True)]
    dot_general x16 -> x0, matrix products: 19.9 us -> none  [the longest x3 3.69 us: panel_factor(): jnp.dot(new_left, coupling.T, precision=lax.Precision.HIGHEST)]
    all_to_all x1 -> x0, blocking collectives: 11.5 us -> none  [on_device(): lax.all_to_all(factor, 'narrow', split_axis=1, concat_axis=0, tiled=True)]
    gather x2 -> x0, local copies, waits for them, and re-layouts: 4.78 us -> none  [the longest x1 2.67 us: on_device(): earlier[piv_local].astype(jnp.float32)]
  transfers between devices with their start and end apart: 2 -> 0, of which waited for: 2 -> 0; matrix products, arithmetic and copies ran while one was open for 2% -> 0% of each run, Pallas kernels for 0% -> 0%
where the time goes in v1:
time: 99.3 us; the launch traced here: 99.1 us
  Pallas kernels  95.7 us (96%)
  local copies, waits for them, and re-layouts  3.46 us (3%)
    pallas_call x1, Pallas kernels, on_device(): pl.pallas_call(kernel, out_shape=jax.ShapeDtypeStruct((1024, NPIV // (2 *...  95.7 us

profile of v1, /device:TPU:1, one launch (start us, length us, event | category | flops | bytes accessed | tf_op | source)
XLA Modules:
  0.0 99.1 jit_solution(8550688398472490702)
XLA Ops:
  0.0 1.5 %copy.6.own_col = s32[512,1]{1,0:T(8,128)} copy(s32[512,1]{0,1:T(1,128)} %param.9) | data formatting | bytes 4096 | tf_op args[4]
  1.5 95.7 %shard_map.55 = f32[1024,64]{1,0:T(8,128)} custom-call(bf16[4,2,128,1152]{3,2,1,0:T(8,128)(2,1)} %bitcast.5, bf16[4,2,128,256]{3,2,1,0:T(8,128)(2,1)} %bitcast.6, f32[4,128,128]{2,1,0:T(8,128)} %inv.1, s32[512,1]{1,0:T(8,128)} %copy.6.own_col, s32[1,512]{1,0:T(1,128)} %bitcast.4, s32[1,512]{1,0:T(1,128)} %bitcast.7), custom_call_target="tpu_custom_call" | custom-call | flops 4000000000 | bytes 4000000 | tf_op jit(solution)/shard_map/pallas_call | solution.py:286
  97.2 1.9 %copy.7 = f32[1024,64]{0,1:T(8,128)} copy(f32[1024,64]{1,0:T(8,128)} %shard_map.55) | data formatting | bytes 524288 | tf_op jit(solution)/shard_map/pallas_call | solution.py:286

commit v2 on v0

v2 whole, which is shorter than its diff:
```python
import jax
import jax.numpy as jnp
from jax import lax
from jax.experimental import pallas as pl
from jax.experimental.pallas import tpu as pltpu
from jax.sharding import PartitionSpec as P

MESH = pl.DeviceIdType.MESH
F32 = jnp.float32
BF16 = jnp.bfloat16
HIGH = lax.Precision.HIGHEST

NPIV = 512
BLK = 128
NBLK = 4
NY = 4
NZ = 16
NX = 4
CAP = 24
SLOT = 32
GROUP = CAP * NY
PIECES = 3
QCOL = PIECES * 128
LOW = ((1, 0), (2, 0), (2, 1), (3, 0), (3, 1), (3, 2))
STEPS = NZ // 4


def dot(a, b, precision=None):
    return lax.dot_general(a, b, (((1,), (0,)), ((), ())), precision=precision, preferred_element_type=F32)


def dot_nt(a, b, precision=None):
    return lax.dot_general(a, b, (((1,), (1,)), ((), ())), precision=precision, preferred_element_type=F32)


def ones_where(cond):
    return jnp.where(cond, 1.0, 0.0).astype(F32)


def iota(shape, dim):
    return lax.broadcasted_iota(jnp.int32, shape, dim)


def kernel(coeffs_in, earlier_in, inv, own_row, loc_row, out,
           coeffs, earlier, sel, ygot, ring, rows, hot,
           diag, diag_core, diag_sum, diag_x, diag_y, diag_all,
           part_send, part_got, part_sum, x_got, made, got,
           ins, y1s, y1r, zs, zr, y2s, y2r, d1s, d1r, d2s, d2r, d3s, d3r, d4s, d4r, d5s, d5r,
           pcs, pcr, xas, xar, os_, or_):
    wide = lax.axis_index("wide")
    narrow = lax.axis_index("narrow")
    z, y = wide // NY, wide % NY
    x, core = narrow // 2, narrow % 2
    other = 1 - core
    ys = [(y + d) % NY for d in (1, 3, 2)]
    xs = [(x + d) % NX for d in (1, 3, 2)]

    def at(zz=z, yy=y, xx=x, cc=core):
        return {"wide": zz * NY + yy, "narrow": xx * 2 + cc}

    def remote(src, dst, send_sem, recv_sem, device):
        return pltpu.make_async_remote_copy(
            src_ref=src, dst_ref=dst, send_sem=send_sem, recv_sem=recv_sem,
            device_id=device, device_id_type=MESH)

    def start(copies):
        for copy in copies:
            copy.start()

    def arrive(copies):
        for copy in copies:
            copy.wait_recv()

    sent = []

    barrier = pltpu.get_barrier_semaphore()
    peers = [at(zz=(z + d) % NZ) for d in (1, 2, NZ - 1, NZ - 2)] + [at(cc=other)]
    peers += [at(yy=v) for v in ys]
    peers += [at(xx=v, cc=c) for v in xs for c in (core, other)]
    for peer in peers:
        pl.semaphore_signal(barrier, inc=1, device_id=peer, device_id_type=MESH)
    fetch = [pltpu.make_async_copy(coeffs_in, coeffs, ins.at[0]), pltpu.make_async_copy(earlier_in, earlier, ins.at[1])]
    start(fetch)

    owners = own_row[...]
    up, along = iota((NPIV, NPIV), 0), iota((NPIV, NPIV), 1)
    owner_col = jnp.sum(jnp.where(up == along, owners.astype(F32), 0.0), axis=1, keepdims=True).astype(jnp.int32)
    before, after = up < along, along < up
    same_owner = owner_col == owners
    slot_row = jnp.sum(ones_where(before & same_owner), axis=0, keepdims=True)
    held = (iota((SLOT, NPIV), 0).astype(F32) == slot_row) & (owners == wide)
    place = jnp.sum(jnp.where(held, loc_row[...].astype(F32) + 1.0, 0.0), axis=1, keepdims=True) - 1.0
    pick = ones_where(iota((SLOT, 1024), 1).astype(F32) == place).astype(BF16)

    z_row, z_col = owners // NY, owner_col // NY
    same_z = z_col == z_row
    rank_row = jnp.sum(ones_where(before & same_z), axis=0, keepdims=True)
    rank_col = jnp.sum(ones_where(after & same_z), axis=1, keepdims=True)
    slot_col = jnp.sum(ones_where(after & same_owner), axis=1, keepdims=True)
    to_rank = ones_where((iota((GROUP, NPIV), 0).astype(F32) == rank_row) & (z_row == z)).astype(BF16)
    source = (owner_col % NY * SLOT).astype(F32) + slot_col
    from_slot = ones_where((iota((NPIV, NY * SLOT), 1).astype(F32) == source) & (z_col == z)).astype(BF16)
    compact = dot(to_rank, from_slot).astype(BF16)
    target = (z_col * GROUP).astype(F32) + rank_col
    hot[...] = ones_where(iota((NPIV, NZ * GROUP), 1).astype(F32) == target).astype(BF16)

    n_coeff, n_early = coeffs.shape[-1], earlier.shape[-1]
    for copy in fetch:
        copy.wait()
    sel[:, :n_coeff] = dot(pick, coeffs[...].reshape(1024, n_coeff)).astype(BF16)
    sel[:, n_coeff:n_coeff + n_early] = dot(pick, earlier[...].reshape(1024, n_early)).astype(BF16)
    rest = NY * QCOL - n_coeff - n_early
    sel[:, n_coeff + n_early:] = jnp.zeros((SLOT, rest), BF16)

    pl.semaphore_wait(barrier, len(peers))

    def quarter(v):
        return pl.ds(pl.multiple_of(v * QCOL, 128), QCOL)

    spread = [remote(sel.at[:, quarter(v)], ygot.at[y], y1s.at[i], y1r.at[i], at(yy=v)) for i, v in enumerate(ys)]
    start(spread)
    sent += spread
    ygot[y] = sel[:, quarter(y)]
    arrive(spread)
    chunk = dot(compact, ygot[...].reshape(NY * SLOT, QCOL)).astype(BF16)

    def chunk_rows(v):
        return pl.ds(pl.multiple_of(v * GROUP, 16), GROUP)

    for g in range(PIECES):
        ring[g, chunk_rows(z), :] = chunk[:, g * 128:(g + 1) * 128]

    def ring_copy(way, step, g, far):
        sign = 1 if way == 0 else NZ - 1
        origin = (z + (NZ - sign) * 2 * (step - 1)) % NZ
        ref = ring.at[g, chunk_rows(origin), :]
        return remote(ref, ref, zs.at[way, step - 1, g, far], zr.at[way, step - 1, g, far],
                      at(zz=(z + sign * (1 + far)) % NZ))

    hops = {}
    for g in range(PIECES):
        for way in (0, 1):
            for step in range(1, STEPS + 1):
                hops[way, step, g, 0] = ring_copy(way, step, g, 0)
                if step < STEPS or way == g % 2:
                    hops[way, step, g, 1] = ring_copy(way, step, g, 1)
    for step in range(1, STEPS + 1):
        for g in range(PIECES):
            for way in (0, 1):
                if step > 1:
                    hops[way, step - 1, g, 1].wait_recv()
                for far in (1, 0):
                    if (way, step, g, far) in hops:
                        hops[way, step, g, far].start()
    sent += list(hops.values())

    def column(v, g):
        return pl.ds(pl.multiple_of(v * QCOL + g * 128, 128), 128)

    for g in range(PIECES):
        for (way, step, gg, far), copy in hops.items():
            if gg == g and (far == 0 or step == STEPS):
                copy.wait_recv()
        rows[:, column(y, g)] = dot(hot[...], ring[g]).astype(BF16)

    def y_send(b):
        ref = rows.at[pl.ds(b * BLK, BLK), quarter(y)]
        copies = [remote(ref, ref, y2s.at[b, i], y2r.at[b, i], at(yy=v)) for i, v in enumerate(ys)]
        start(copies)
        return copies

    y_copies = [y_send(0), y_send(1)]

    mine = rows[:, quarter(y)]
    gain = jnp.where(y == NY - 1, -1.0, 1.0).astype(F32)
    for b in (1, 2, 3):
        value = dot_nt(mine[b * BLK:(b + 1) * BLK], mine[:b * BLK]) * gain
        for c in range(b):
            diag[LOW.index((b, c))] = value[:, c * BLK:(c + 1) * BLK]
    d1 = remote(diag.at[pl.ds(other * 3, 3)], diag_core, d1s, d1r, at(cc=other))
    d1.start()

    def few_rows(v):
        return pl.ds(pl.multiple_of(v * 32, 32), 32)

    d1.wait_recv()
    diag_sum[...] = diag[pl.ds(core * 3, 3)] + diag_core[...]
    d2 = [remote(diag_sum.at[:, few_rows(v)], diag_x.at[x], d2s.at[i], d2r.at[i], at(xx=v)) for i, v in enumerate(xs)]
    start(d2)
    diag_x[x] = diag_sum[:, few_rows(x)]
    y_copies += [y_send(2), y_send(3)]
    sent += [d1] + d2
    for copies in y_copies:
        sent += copies

    def density(b, c):
        block = rows[b * BLK:(b + 1) * BLK, :]
        left = dot_nt(block[:, :n_coeff], coeffs[:, c].reshape(NX * BLK, n_coeff))
        return left - dot_nt(block[:, n_coeff:n_coeff + n_early], earlier[:, c].reshape(NX * BLK, n_early))

    core_copies = []

    def to_core(b):
        arrive(y_copies[b])
        part_send[b] = density(b, other)
        copy = remote(part_send.at[b], part_got.at[b], pcs.at[b], pcr.at[b], at(cc=other))
        copy.start()
        core_copies.append(copy)
        part_sum[b] = density(b, core)

    def chip(v):
        return pl.ds(pl.multiple_of(v * BLK, BLK), BLK)

    x_copies = []

    def to_x(b):
        core_copies[b].wait_recv()
        part_sum[b] = part_sum[b] + part_got[b]
        copies = [remote(part_sum.at[b, :, chip(v)], x_got.at[b, i], xas.at[b, i], xar.at[b, i], at(xx=v))
                  for i, v in enumerate(xs)]
        start(copies)
        x_copies.append(copies)

    low = {}
    new = []
    home = [(x, other)] + [(v, c) for v in xs for c in (core, other)]

    def finish(b):
        arrive(x_copies[b])
        rest_rows = part_sum[b, :, chip(x)] + x_got[b, 0] + x_got[b, 1] + x_got[b, 2]
        for d in range(b):
            rest_rows = rest_rows - dot(low[b, d], new[d], HIGH)
        value = dot(inv[b].T, rest_rows, HIGH)
        new.append(value)
        made[b] = value
        for c in (0, 1):
            @pl.when((x != b) | (core != c))
            def _():
                out_copy(b, c).start()

            @pl.when((x == b) & (core == c))
            def _():
                got[:, chip(narrow)] = value[c * 64:(c + 1) * 64]

    def out_copy(b, c):
        return remote(made.at[b, pl.ds(c * 64, 64)], got.at[:, chip(narrow)], os_.at[b, c], or_.at[narrow], at(xx=b, cc=c))

    to_core(0)
    arrive(d2)
    diag_y[y] = diag_x[0] + diag_x[1] + diag_x[2] + diag_x[3]
    d3 = [remote(diag_y.at[y], diag_y.at[y], d3s.at[i], d3r.at[i], at(yy=v)) for i, v in enumerate(ys)]
    start(d3)
    to_x(0)
    to_core(1)
    to_x(1)
    arrive(d3)
    diag_all[pl.ds(core * 3, 3), few_rows(x)] = diag_y[0] + diag_y[1] + diag_y[2] + diag_y[3]
    spot = diag_all.at[pl.ds(core * 3, 3), few_rows(x)]
    d4 = [remote(spot, spot, d4s.at[i], d4r.at[i], at(xx=v)) for i, v in enumerate(xs)]
    start(d4)
    to_core(2)
    to_x(2)
    finish(0)
    arrive(d4)
    half = diag_all.at[pl.ds(core * 3, 3)]
    d5 = remote(half, half, d5s, d5r, at(cc=other))
    d5.start()
    to_core(3)
    to_x(3)
    d5.wait_recv()

    for c in range(3):
        below = list(range(c + 1, 4))
        rest_rows = jnp.concatenate([diag_all[LOW.index((b, c))] for b in below], axis=0)
        for d in range(c):
            rest_rows = rest_rows - dot_nt(jnp.concatenate([low[b, d] for b in below], axis=0), low[c, d], HIGH)
        solved = dot(rest_rows, inv[c], HIGH)
        for i, b in enumerate(below):
            low[b, c] = solved[i * BLK:(i + 1) * BLK]
    for b in (1, 2, 3):
        finish(b)

    for xx, cc in home:
        source_n = xx * 2 + cc
        remote(made.at[0, pl.ds(0, 64)], got.at[:, chip(source_n)], os_.at[0, 0], or_.at[source_n], at(xx=xx, cc=cc)).wait_recv()
    out[...] = got[...]

    for b in range(NBLK):
        for c in (0, 1):
            @pl.when((x != b) | (core != c))
            def _():
                out_copy(b, c).wait_send()
    sent += d3 + d4 + [d5] + core_copies
    for copies in x_copies:
        sent += copies
    for copy in sent:
        copy.wait_send()


def on_device(coeffs, earlier, inv_tiles, piv_local, piv_owner):
    n_coeff, n_early = coeffs.shape[1], earlier.shape[1]
    dma = pltpu.SemaphoreType.DMA
    vmem = pltpu.VMEM
    in_vmem = pl.BlockSpec(memory_space=pltpu.VMEM)
    anywhere = pl.BlockSpec(memory_space=pl.ANY)
    result = pl.pallas_call(
        kernel,
        out_shape=jax.ShapeDtypeStruct((NPIV // (2 * NX), 1024), F32),
        in_specs=[anywhere, anywhere, in_vmem, in_vmem, in_vmem],
        out_specs=in_vmem,
        scratch_shapes=[
            vmem((NX, 2, BLK, n_coeff), BF16),
            vmem((NX, 2, BLK, n_early), BF16),
            vmem((SLOT, NY * QCOL), BF16),
            vmem((NY, SLOT, QCOL), BF16),
            vmem((PIECES, NZ * GROUP, 128), BF16),
            vmem((NPIV, NY * QCOL), BF16),
            vmem((NPIV, NZ * GROUP), BF16),
            vmem((6, BLK, BLK), F32),
            vmem((3, BLK, BLK), F32),
            vmem((3, BLK, BLK), F32),
            vmem((NX, 3, 32, BLK), F32),
            vmem((NY, 3, 32, BLK), F32),
            vmem((6, BLK, BLK), F32),
            vmem((NBLK, BLK, NX * BLK), F32),
            vmem((NBLK, BLK, NX * BLK), F32),
            vmem((NBLK, BLK, NX * BLK), F32),
            vmem((NBLK, 3, BLK, BLK), F32),
            vmem((NBLK, BLK, BLK), F32),
            vmem((64, 1024), F32),
            dma((2,)),
            dma((3,)), dma((3,)),
            dma((2, STEPS, PIECES, 2)), dma((2, STEPS, PIECES, 2)),
            dma((NBLK, 3)), dma((NBLK, 3)),
            dma, dma,
            dma((3,)), dma((3,)),
            dma((3,)), dma((3,)),
            dma((3,)), dma((3,)),
            dma, dma,
            dma((NBLK,)), dma((NBLK,)),
            dma((NBLK, 3)), dma((NBLK, 3)),
            dma((NBLK, 2)), dma((2 * NX,)),
        ],
        compiler_params=pltpu.CompilerParams(
            collective_id=0, has_side_effects=True, vmem_limit_bytes=56 * 1024 * 1024),
        cost_estimate=pl.CostEstimate(flops=4_000_000_000, bytes_accessed=4_000_000, transcendentals=0),
    )(coeffs.reshape(NX, 2, BLK, n_coeff), earlier.reshape(NX, 2, BLK, n_early), inv_tiles,
      piv_owner.reshape(1, NPIV), piv_local.reshape(1, NPIV))
    return result.T


def solution(mesh):
    return jax.shard_map(
        on_device,
        mesh=mesh,
        in_specs=(P("wide", "narrow"), P("wide", "narrow"), P(), P(), P()),
        out_specs=P("wide", "narrow"),
        check_vma=False,
    )
```

time: 477 us -> 80.3 us (0.17)
  blocking collectives: 277 us -> 0 us
  waiting for transfers between devices: 156 us -> 0 us
  Pallas kernels: 0 us -> 78.4 us
  matrix products: 19.9 us -> 0 us
  between operations: 13.5 us -> 0.01 us
    psum x1 -> x0, blocking collectives: 266 us -> none  [on_device(): lax.psum((pick_coeffs, pick_earlier), 'wide')]
    psum x1 -> x0, waiting for transfers between devices: 118 us -> none  [on_device(): diag_block = lax.psum(diag_part, 'narrow')]
    pallas_call x0 -> x1, Pallas kernels: none -> 78.4 us  [on_device(): pl.pallas_call(kernel, out_shape=jax.ShapeDtypeStruct((NPIV // (2 * NX),...]
    reduce_scatter x1 -> x0, waiting for transfers between devices: 37.6 us -> none  [on_device(): lax.psum_scatter(partial_value, 'narrow', scatter_dimension=0, tiled=True)]
    dot_general x16 -> x0, matrix products: 19.9 us -> none  [the longest x3 3.69 us: panel_factor(): jnp.dot(new_left, coupling.T, precision=lax.Precision.HIGHEST)]
    all_to_all x1 -> x0, blocking collectives: 11.5 us -> none  [on_device(): lax.all_to_all(factor, 'narrow', split_axis=1, concat_axis=0, tiled=True)]
    gather x2 -> x0, local copies, waits for them, and re-layouts: 4.78 us -> none  [the longest x1 2.67 us: on_device(): earlier[piv_local].astype(jnp.float32)]
  transfers between devices with their start and end apart: 2 -> 0, of which waited for: 2 -> 0; matrix products, arithmetic and copies ran while one was open for 2% -> 0% of each run, Pallas kernels for 0% -> 0%
where the time goes in v2:
time: 80.3 us; the launch traced here: 80.1 us
  Pallas kernels  78.4 us (98%)
  local copies, waits for them, and re-layouts  1.67 us (2%)
    pallas_call x1, Pallas kernels, on_device(): pl.pallas_call(kernel, out_shape=jax.ShapeDtypeStruct((NPIV // (2 * NX),...  78.4 us
    unnamed x1, local copies, waits for them, and re-layouts  1.67 us

profile of v2, /device:TPU:1, one launch (start us, length us, event | category | flops | bytes accessed | tf_op | source)
XLA Modules:
  0.0 80.1 jit_solution(12056280833476113924)
XLA Ops:
  0.0 78.4 %shard_map.55 = f32[64,1024]{1,0:T(8,128)} custom-call(bf16[4,2,128,1152]{3,2,1,0:T(8,128)(2,1)} %bitcast.6, bf16[4,2,128,256]{3,2,1,0:T(8,128)(2,1)} %bitcast.7, f32[4,128,128]{2,1,0:T(8,128)} %inv.1, s32[1,512]{1,0:T(1,128)} %bitcast.8, s32[1,512]{1,0:T(1,128)} %bitcast.9), custom_call_target="tpu_custom_call" | custom-call | flops 4000000000 | bytes 4000000 | tf_op jit(solution)/shard_map/pallas_call | solution.py:306
  78.4 1.7 %copy.7 = f32[1024,64]{0,1:T(8,128)} copy(f32[1024,64]{0,1:T(8,128)} %bitcast.5) | data formatting | bytes 524288

commit v3 on v2

--- a/solution.py
+++ b/solution.py
@@ -19,9 +19,12 @@
 CAP = 24
 SLOT = 32
 GROUP = CAP * NY
-PIECES = 3
-QCOL = PIECES * 128
+QCOL = 384
+PARTS = ((0, 128), (128, 256))
+LAG = (0, 0)
 LOW = ((1, 0), (2, 0), (2, 1), (3, 0), (3, 1), (3, 2))
+CHUNK = 64
+WINDOW = 3
 STEPS = NZ // 4
 
 
@@ -42,9 +45,9 @@
 
 
 def kernel(coeffs_in, earlier_in, inv, own_row, loc_row, out,
-           coeffs, earlier, sel, ygot, ring, rows, hot,
+           coeffs, earlier, inv_t, sel, ygot, ring_a, ring_b, rows, hot,
            diag, diag_core, diag_sum, diag_x, diag_y, diag_all,
-           part_send, part_got, part_sum, x_got, made, got,
+           part_send, part_got, part_sum, x_got, made,
            ins, y1s, y1r, zs, zr, y2s, y2r, d1s, d1r, d2s, d2r, d3s, d3r, d4s, d4r, d5s, d5r,
            pcs, pcr, xas, xar, os_, or_):
     wide = lax.axis_index("wide")
@@ -104,6 +107,9 @@
     target = (z_col * GROUP).astype(F32) + rank_col
     hot[...] = ones_where(iota((NPIV, NZ * GROUP), 1).astype(F32) == target).astype(BF16)
 
+    for b in range(NBLK):
+        inv_t[b] = inv[b].T
+    rings = (ring_a, ring_b)
     n_coeff, n_early = coeffs.shape[-1], earlier.shape[-1]
     for copy in fetch:
         copy.wait()
@@ -127,49 +133,78 @@
     def chunk_rows(v):
         return pl.ds(pl.multiple_of(v * GROUP, 16), GROUP)
 
-    for g in range(PIECES):
-        ring[g, chunk_rows(z), :] = chunk[:, g * 128:(g + 1) * 128]
+    for g, (low_col, width) in enumerate(PARTS):
+        rings[g][chunk_rows(z), :] = chunk[:, low_col:low_col + width]
 
     def ring_copy(way, step, g, far):
         sign = 1 if way == 0 else NZ - 1
         origin = (z + (NZ - sign) * 2 * (step - 1)) % NZ
-        ref = ring.at[g, chunk_rows(origin), :]
+        ref = rings[g].at[chunk_rows(origin), :]
         return remote(ref, ref, zs.at[way, step - 1, g, far], zr.at[way, step - 1, g, far],
                       at(zz=(z + sign * (1 + far)) % NZ))
 
     hops = {}
-    for g in range(PIECES):
+    for g in range(len(PARTS)):
         for way in (0, 1):
             for step in range(1, STEPS + 1):
                 hops[way, step, g, 0] = ring_copy(way, step, g, 0)
                 if step < STEPS or way == g % 2:
                     hops[way, step, g, 1] = ring_copy(way, step, g, 1)
-    for step in range(1, STEPS + 1):
-        for g in range(PIECES):
+    sent += list(hops.values())
+
+    def columns(v, g):
+        return pl.ds(pl.multiple_of(v * QCOL + PARTS[g][0], 128), PARTS[g][1])
+
+    def ring_tick(tick):
+        for g in range(len(PARTS)):
+            step = tick - LAG[g]
             for way in (0, 1):
-                if step > 1:
+                if 1 < step <= STEPS:
                     hops[way, step - 1, g, 1].wait_recv()
                 for far in (1, 0):
                     if (way, step, g, far) in hops:
                         hops[way, step, g, far].start()
-    sent += list(hops.values())
-
-    def column(v, g):
-        return pl.ds(pl.multiple_of(v * QCOL + g * 128, 128), 128)
-
-    for g in range(PIECES):
+
+    def gathered(g):
         for (way, step, gg, far), copy in hops.items():
             if gg == g and (far == 0 or step == STEPS):
                 copy.wait_recv()
-        rows[:, column(y, g)] = dot(hot[...], ring[g]).astype(BF16)
-
-    def y_send(b):
-        ref = rows.at[pl.ds(b * BLK, BLK), quarter(y)]
-        copies = [remote(ref, ref, y2s.at[b, i], y2r.at[b, i], at(yy=v)) for i, v in enumerate(ys)]
-        start(copies)
-        return copies
-
-    y_copies = [y_send(0), y_send(1)]
+        rows[:, columns(y, g)] = dot(hot[...], rings[g][...]).astype(BF16)
+
+    for tick in range(1, STEPS + LAG[1] + 1):
+        ring_tick(tick)
+    last_width = n_coeff + n_early - (NY - 1) * QCOL
+    n_chunk = NPIV // CHUNK
+
+    def y_copies(q, width):
+        ref = rows.at[pl.ds(q * CHUNK, CHUNK), pl.ds(pl.multiple_of(y * QCOL, 128), width)]
+        return [remote(ref, ref, y2s.at[q, i], y2r.at[q, i], at(yy=v)) for i, v in enumerate(ys)]
+
+    def by_width(from_y, act):
+        @pl.when(from_y != NY - 1)
+        def _():
+            act(QCOL)
+
+        @pl.when(from_y == NY - 1)
+        def _():
+            act(last_width)
+
+    def y_send(q):
+        by_width(y, lambda width: start(y_copies(q, width)))
+
+    def y_sent(q):
+        by_width(y, lambda width: [copy.wait_send() for copy in y_copies(q, width)])
+
+    def y_arrive(q):
+        for i, d in enumerate((1, 3, 2)):
+            by_width((y + NY - d) % NY, lambda width: y_copies(q, width)[i].wait_recv())
+        if q + WINDOW < n_chunk:
+            y_send(q + WINDOW)
+
+    gathered(0)
+    gathered(1)
+    for q in range(WINDOW):
+        y_send(q)
 
     mine = rows[:, quarter(y)]
     gain = jnp.where(y == NY - 1, -1.0, 1.0).astype(F32)
@@ -188,20 +223,18 @@
     d2 = [remote(diag_sum.at[:, few_rows(v)], diag_x.at[x], d2s.at[i], d2r.at[i], at(xx=v)) for i, v in enumerate(xs)]
     start(d2)
     diag_x[x] = diag_sum[:, few_rows(x)]
-    y_copies += [y_send(2), y_send(3)]
     sent += [d1] + d2
-    for copies in y_copies:
-        sent += copies
 
     def density(b, c):
         block = rows[b * BLK:(b + 1) * BLK, :]
-        left = dot_nt(block[:, :n_coeff], coeffs[:, c].reshape(NX * BLK, n_coeff))
-        return left - dot_nt(block[:, n_coeff:n_coeff + n_early], earlier[:, c].reshape(NX * BLK, n_early))
+        left = dot_nt(coeffs[:, c].reshape(NX * BLK, n_coeff), block[:, :n_coeff])
+        return left - dot_nt(earlier[:, c].reshape(NX * BLK, n_early), block[:, n_coeff:n_coeff + n_early])
 
     core_copies = []
 
     def to_core(b):
-        arrive(y_copies[b])
+        for q in range(b * BLK // CHUNK, (b + 1) * BLK // CHUNK):
+            y_arrive(q)
         part_send[b] = density(b, other)
         copy = remote(part_send.at[b], part_got.at[b], pcs.at[b], pcr.at[b], at(cc=other))
         copy.start()
@@ -216,7 +249,7 @@
     def to_x(b):
         core_copies[b].wait_recv()
         part_sum[b] = part_sum[b] + part_got[b]
-        copies = [remote(part_sum.at[b, :, chip(v)], x_got.at[b, i], xas.at[b, i], xar.at[b, i], at(xx=v))
+        copies = [remote(part_sum.at[b, chip(v)], x_got.at[b, i], xas.at[b, i], xar.at[b, i], at(xx=v))
                   for i, v in enumerate(xs)]
         start(copies)
         x_copies.append(copies)
@@ -224,13 +257,16 @@
     low = {}
     new = []
     home = [(x, other)] + [(v, c) for v in xs for c in (core, other)]
+    less = {}
 
     def finish(b):
         arrive(x_copies[b])
-        rest_rows = part_sum[b, :, chip(x)] + x_got[b, 0] + x_got[b, 1] + x_got[b, 2]
+        rest_rows = (part_sum[b, chip(x)] + x_got[b, 0] + x_got[b, 1] + x_got[b, 2]).T
         for d in range(b):
-            rest_rows = rest_rows - dot(low[b, d], new[d], HIGH)
-        value = dot(inv[b].T, rest_rows, HIGH)
+            rest_rows = rest_rows - less[d][(b - d - 1) * BLK:(b - d) * BLK]
+        value = dot(inv_t[b], rest_rows, HIGH)
+        if b in low:
+            less[b] = dot(low[b], value, HIGH)
         new.append(value)
         made[b] = value
         for c in (0, 1):
@@ -240,10 +276,13 @@
 
             @pl.when((x == b) & (core == c))
             def _():
-                got[:, chip(narrow)] = value[c * 64:(c + 1) * 64]
+                own_copy(b, c).start()
+
+    def own_copy(b, c):
+        return pltpu.make_async_copy(made.at[b, pl.ds(c * 64, 64)], out.at[:, chip(narrow)], ins.at[2])
 
     def out_copy(b, c):
-        return remote(made.at[b, pl.ds(c * 64, 64)], got.at[:, chip(narrow)], os_.at[b, c], or_.at[narrow], at(xx=b, cc=c))
+        return remote(made.at[b, pl.ds(c * 64, 64)], out.at[:, chip(narrow)], os_.at[b, c], or_.at[narrow], at(xx=b, cc=c))
 
     to_core(0)
     arrive(d2)
@@ -270,27 +309,30 @@
     d5.wait_recv()
 
     for c in range(3):
-        below = list(range(c + 1, 4))
-        rest_rows = jnp.concatenate([diag_all[LOW.index((b, c))] for b in below], axis=0)
+        rest_rows = jnp.concatenate([diag_all[LOW.index((b, c))] for b in range(c + 1, NBLK)], axis=0)
         for d in range(c):
-            rest_rows = rest_rows - dot_nt(jnp.concatenate([low[b, d] for b in below], axis=0), low[c, d], HIGH)
-        solved = dot(rest_rows, inv[c], HIGH)
-        for i, b in enumerate(below):
-            low[b, c] = solved[i * BLK:(i + 1) * BLK]
+            skip = (c - d) * BLK
+            rest_rows = rest_rows - dot_nt(low[d][skip:], low[d][skip - BLK:skip], HIGH)
+        low[c] = dot(rest_rows, inv[c], HIGH)
+    less[0] = dot(low[0], new[0], HIGH)
     for b in (1, 2, 3):
         finish(b)
 
     for xx, cc in home:
         source_n = xx * 2 + cc
-        remote(made.at[0, pl.ds(0, 64)], got.at[:, chip(source_n)], os_.at[0, 0], or_.at[source_n], at(xx=xx, cc=cc)).wait_recv()
-    out[...] = got[...]
-
+        remote(made.at[0, pl.ds(0, 64)], out.at[:, chip(source_n)], os_.at[0, 0], or_.at[source_n], at(xx=xx, cc=cc)).wait_recv()
     for b in range(NBLK):
         for c in (0, 1):
             @pl.when((x != b) | (core != c))
             def _():
                 out_copy(b, c).wait_send()
+
+            @pl.when((x == b) & (core == c))
+            def _():
+                own_copy(b, c).wait()
     sent += d3 + d4 + [d5] + core_copies
+    for q in range(n_chunk):
+        y_sent(q)
     for copies in x_copies:
         sent += copies
     for copy in sent:
@@ -307,13 +349,15 @@
         kernel,
         out_shape=jax.ShapeDtypeStruct((NPIV // (2 * NX), 1024), F32),
         in_specs=[anywhere, anywhere, in_vmem, in_vmem, in_vmem],
-        out_specs=in_vmem,
+        out_specs=anywhere,
         scratch_shapes=[
             vmem((NX, 2, BLK, n_coeff), BF16),
             vmem((NX, 2, BLK, n_early), BF16),
+            vmem((NBLK, BLK, BLK), F32),
             vmem((SLOT, NY * QCOL), BF16),
             vmem((NY, SLOT, QCOL), BF16),
-            vmem((PIECES, NZ * GROUP, 128), BF16),
+            vmem((NZ * GROUP, PARTS[0][1]), BF16),
+            vmem((NZ * GROUP, PARTS[1][1]), BF16),
             vmem((NPIV, NY * QCOL), BF16),
             vmem((NPIV, NZ * GROUP), BF16),
             vmem((6, BLK, BLK), F32),
@@ -322,16 +366,15 @@
             vmem((NX, 3, 32, BLK), F32),
             vmem((NY, 3, 32, BLK), F32),
             vmem((6, BLK, BLK), F32),
-            vmem((NBLK, BLK, NX * BLK), F32),
-            vmem((NBLK, BLK, NX * BLK), F32),
-            vmem((NBLK, BLK, NX * BLK), F32),
+            vmem((NBLK, NX * BLK, BLK), F32),
+            vmem((NBLK, NX * BLK, BLK), F32),
+            vmem((NBLK, NX * BLK, BLK), F32),
             vmem((NBLK, 3, BLK, BLK), F32),
             vmem((NBLK, BLK, BLK), F32),
-            vmem((64, 1024), F32),
-            dma((2,)),
+            dma((3,)),
             dma((3,)), dma((3,)),
-            dma((2, STEPS, PIECES, 2)), dma((2, STEPS, PIECES, 2)),
-            dma((NBLK, 3)), dma((NBLK, 3)),
+            dma((2, STEPS, len(PARTS), 2)), dma((2, STEPS, len(PARTS), 2)),
+            dma((NPIV // CHUNK, 3)), dma((NPIV // CHUNK, 3)),
             dma, dma,
             dma((3,)), dma((3,)),
             dma((3,)), dma((3,)),

time: 80.3 us -> 75.9 us (0.945)
  Pallas kernels: 78.4 us -> 73.5 us
    pallas_call x1, Pallas kernels: 78.4 us -> 73.5 us  [on_device(): pl.pallas_call(kernel, out_shape=jax.ShapeDtypeStruct((NPIV // (2 * NX),...]
where the time goes in v3:
time: 75.9 us; the launch traced here: 75.2 us
  Pallas kernels  73.5 us (97%)
  local copies, waits for them, and re-layouts  1.67 us (2%)
    pallas_call x1, Pallas kernels, on_device(): pl.pallas_call(kernel, out_shape=jax.ShapeDtypeStruct((NPIV // (2 * NX),...  73.5 us
    unnamed x1, local copies, waits for them, and re-layouts  1.67 us

profile of v3, /device:TPU:1, one launch (start us, length us, event | category | flops | bytes accessed | tf_op | source)
XLA Modules:
  0.0 75.2 jit_solution(9501388278378358460)
XLA Ops:
  0.0 73.5 %shard_map.55 = f32[64,1024]{1,0:T(8,128)} custom-call(bf16[4,2,128,1152]{3,2,1,0:T(8,128)(2,1)} %bitcast.6, bf16[4,2,128,256]{3,2,1,0:T(8,128)(2,1)} %bitcast.7, f32[4,128,128]{2,1,0:T(8,128)} %inv.1, s32[1,512]{1,0:T(1,128)} %bitcast.8, s32[1,512]{1,0:T(1,128)} %bitcast.9), custom_call_target="tpu_custom_call" | custom-call | flops 4000000000 | bytes 4000000 | tf_op jit(solution)/shard_map/pallas_call | solution.py:348
  73.5 1.7 %copy.7 = f32[1024,64]{0,1:T(8,128)} copy(f32[1024,64]{0,1:T(8,128)} %bitcast.5) | data formatting | bytes 524288

commit v4 on v3

--- a/solution.py
+++ b/solution.py
@@ -23,6 +23,7 @@
 PARTS = ((0, 128), (128, 256))
 LAG = (0, 0)
 LOW = ((1, 0), (2, 0), (2, 1), (3, 0), (3, 1), (3, 2))
+SIZES = (128, 128, 128, 128)
 CHUNK = 64
 WINDOW = 3
 STEPS = NZ // 4
@@ -55,8 +56,8 @@
     z, y = wide // NY, wide % NY
     x, core = narrow // 2, narrow % 2
     other = 1 - core
-    ys = [(y + d) % NY for d in (1, 3, 2)]
-    xs = [(x + d) % NX for d in (1, 3, 2)]
+    ys = [(y + d) % NY for d in (2, 1, 3)]
+    xs = [(x + d) % NX for d in (2, 1, 3)]
 
     def at(zz=z, yy=y, xx=x, cc=core):
         return {"wide": zz * NY + yy, "narrow": xx * 2 + cc}
@@ -196,7 +197,7 @@
         by_width(y, lambda width: [copy.wait_send() for copy in y_copies(q, width)])
 
     def y_arrive(q):
-        for i, d in enumerate((1, 3, 2)):
+        for i, d in enumerate((2, 1, 3)):
             by_width((y + NY - d) % NY, lambda width: y_copies(q, width)[i].wait_recv())
         if q + WINDOW < n_chunk:
             y_send(q + WINDOW)
@@ -225,31 +226,36 @@
     diag_x[x] = diag_sum[:, few_rows(x)]
     sent += [d1] + d2
 
-    def density(b, c):
-        block = rows[b * BLK:(b + 1) * BLK, :]
-        left = dot_nt(coeffs[:, c].reshape(NX * BLK, n_coeff), block[:, :n_coeff])
-        return left - dot_nt(earlier[:, c].reshape(NX * BLK, n_early), block[:, n_coeff:n_coeff + n_early])
+    starts = [sum(SIZES[:k]) for k in range(len(SIZES) + 1)]
+
+    def span(k):
+        return pl.ds(starts[k], SIZES[k])
+
+    def density(k, c):
+        block = rows[starts[k]:starts[k + 1], :]
+        left = dot_nt(block[:, :n_coeff], coeffs[:, c].reshape(NX * BLK, n_coeff))
+        return left - dot_nt(block[:, n_coeff:n_coeff + n_early], earlier[:, c].reshape(NX * BLK, n_early))
 
     core_copies = []
 
-    def to_core(b):
-        for q in range(b * BLK // CHUNK, (b + 1) * BLK // CHUNK):
+    def to_core(k):
+        for q in range(starts[k] // CHUNK, starts[k + 1] // CHUNK):
             y_arrive(q)
-        part_send[b] = density(b, other)
-        copy = remote(part_send.at[b], part_got.at[b], pcs.at[b], pcr.at[b], at(cc=other))
+        part_send[span(k)] = density(k, other)
+        copy = remote(part_send.at[span(k)], part_got.at[span(k)], pcs.at[k], pcr.at[k], at(cc=other))
         copy.start()
         core_copies.append(copy)
-        part_sum[b] = density(b, core)
+        part_sum[span(k)] = density(k, core)
 
     def chip(v):
         return pl.ds(pl.multiple_of(v * BLK, BLK), BLK)
 
     x_copies = []
 
-    def to_x(b):
-        core_copies[b].wait_recv()
-        part_sum[b] = part_sum[b] + part_got[b]
-        copies = [remote(part_sum.at[b, chip(v)], x_got.at[b, i], xas.at[b, i], xar.at[b, i], at(xx=v))
+    def to_x(k):
+        core_copies[k].wait_recv()
+        part_sum[span(k)] = part_sum[span(k)] + part_got[span(k)]
+        copies = [remote(part_sum.at[span(k), chip(v)], x_got.at[i, span(k)], xas.at[k, i], xar.at[k, i], at(xx=v))
                   for i, v in enumerate(xs)]
         start(copies)
         x_copies.append(copies)
@@ -260,8 +266,11 @@
     less = {}
 
     def finish(b):
-        arrive(x_copies[b])
-        rest_rows = (part_sum[b, chip(x)] + x_got[b, 0] + x_got[b, 1] + x_got[b, 2]).T
+        for k in range(len(SIZES)):
+            if b * BLK <= starts[k] < (b + 1) * BLK:
+                arrive(x_copies[k])
+        block = pl.ds(b * BLK, BLK)
+        rest_rows = part_sum[block, chip(x)] + x_got[0, block] + x_got[1, block] + x_got[2, block]
         for d in range(b):
             rest_rows = rest_rows - less[d][(b - d - 1) * BLK:(b - d) * BLK]
         value = dot(inv_t[b], rest_rows, HIGH)
@@ -304,8 +313,9 @@
     half = diag_all.at[pl.ds(core * 3, 3)]
     d5 = remote(half, half, d5s, d5r, at(cc=other))
     d5.start()
-    to_core(3)
-    to_x(3)
+    for k in range(3, len(SIZES)):
+        to_core(k)
+        to_x(k)
     d5.wait_recv()
 
     for c in range(3):
@@ -366,10 +376,10 @@
             vmem((NX, 3, 32, BLK), F32),
             vmem((NY, 3, 32, BLK), F32),
             vmem((6, BLK, BLK), F32),
-            vmem((NBLK, NX * BLK, BLK), F32),
-            vmem((NBLK, NX * BLK, BLK), F32),
-            vmem((NBLK, NX * BLK, BLK), F32),
-            vmem((NBLK, 3, BLK, BLK), F32),
+            vmem((NPIV, NX * BLK), F32),
+            vmem((NPIV, NX * BLK), F32),
+            vmem((NPIV, NX * BLK), F32),
+            vmem((3, NPIV, BLK), F32),
             vmem((NBLK, BLK, BLK), F32),
             dma((3,)),
             dma((3,)), dma((3,)),
@@ -380,8 +390,8 @@
             dma((3,)), dma((3,)),
             dma((3,)), dma((3,)),
             dma, dma,
-            dma((NBLK,)), dma((NBLK,)),
-            dma((NBLK, 3)), dma((NBLK, 3)),
+            dma((len(SIZES),)), dma((len(SIZES),)),
+            dma((len(SIZES), 3)), dma((len(SIZES), 3)),
             dma((NBLK, 2)), dma((2 * NX,)),
         ],
         compiler_params=pltpu.CompilerParams(

time: 75.9 us -> 75 us (0.988)
  Pallas kernels: 73.5 us -> 72.6 us
    pallas_call x1, Pallas kernels: 73.5 us -> 72.6 us  [on_device(): pl.pallas_call(kernel, out_shape=jax.ShapeDtypeStruct((NPIV // (2 * NX),...]
where the time goes in v4:
time: 75 us; the launch traced here: 74.3 us
  Pallas kernels  72.6 us (97%)
  local copies, waits for them, and re-layouts  1.67 us (2%)
    pallas_call x1, Pallas kernels, on_device(): pl.pallas_call(kernel, out_shape=jax.ShapeDtypeStruct((NPIV // (2 * NX),...  72.6 us
    unnamed x1, local copies, waits for them, and re-layouts  1.67 us

profile of v4, /device:TPU:1, one launch (start us, length us, event | category | flops | bytes accessed | tf_op | source)
XLA Modules:
  0.0 74.3 jit_solution(14306571321250875003)
XLA Ops:
  0.0 72.6 %shard_map.55 = f32[64,1024]{1,0:T(8,128)} custom-call(bf16[4,2,128,1152]{3,2,1,0:T(8,128)(2,1)} %bitcast.6, bf16[4,2,128,256]{3,2,1,0:T(8,128)(2,1)} %bitcast.7, f32[4,128,128]{2,1,0:T(8,128)} %inv.1, s32[1,512]{1,0:T(1,128)} %bitcast.8, s32[1,512]{1,0:T(1,128)} %bitcast.9), custom_call_target="tpu_custom_call" | custom-call | flops 4000000000 | bytes 4000000 | tf_op jit(solution)/shard_map/pallas_call | solution.py:358
  72.6 1.7 %copy.7 = f32[1024,64]{0,1:T(8,128)} copy(f32[1024,64]{0,1:T(8,128)} %bitcast.5) | data formatting | bytes 524288
